TPU v7x, 32 devices: a whole 2x2x4 slice. The times are simulated.
32 devices in a mesh: parts: 2 (over y), span: 4 (over x, core), seq: 4 (over z).
Axes of the slice: x: 2, y: 2, z: 4, core: 2. Of those that a mesh axis runs over, the one named last changes fastest.
Arguments:
- q_in: bfloat16 [8, 1024, 4096], P(('parts', 'span'), 'seq'), parts along dimension 0, may hold values from -9 to 9
- k_in: bfloat16 [8, 1024, 4096], P(('parts', 'span'), 'seq'), parts along dimension 0, may hold values from -9 to 9
- v_in: bfloat16 [8, 1024, 4096], P(('parts', 'span'), 'seq'), parts along dimension 0, may hold values from -18 to 18
- timesteps: int32 [8], P('parts'), parts along dimension 0, may hold values from 0 to 31
- gate_table: float32 [32, 4096], replicated, may hold values from 0.1 to 1.9
Outputs:
- gated_out: bfloat16 [8, 1024, 4096], P(('parts', 'span'), 'seq'), parts along dimension 0
There are 2 independent parts, one for each index of `parts`. A program takes and returns all parts, laid end to end along the dimension named above; an argument that names none is the same for every part. Nothing has to cross between parts.
All inputs are finite; a program needn't handle non-finite values.
Results may differ from a plain program's by a relative error of at most 0.0053.
Values may be sent and summed in bfloat16 or wider, within the bound.
A program may use at most 128 MiB of HBM per device.

v0:
```python
import math
import jax
import jax.numpy as jnp
from jax import lax
from jax.sharding import PartitionSpec as P

HD = 128
masked_score = -1e30


def local(q_in, k_in, v_in, timesteps, gate_table):
    head_rows, key_rows, value_rows = (
        lax.all_to_all(q_in[0], "seq", split_axis=1, concat_axis=0, tiled=True),
        lax.all_to_all(k_in[0], "seq", split_axis=1, concat_axis=0, tiled=True),
        lax.all_to_all(v_in[0], "seq", split_axis=1, concat_axis=0, tiled=True),
    )
    length = head_rows.shape[0]
    columns = head_rows.shape[1]
    heads = columns // HD
    scale = HD ** (-0.5)
    span_id = lax.axis_index("span")
    limit = (span_id + 1) * length
    query_three = head_rows.reshape(length, heads, HD)
    init = (
        jnp.full((heads, length), masked_score, jnp.float32),
        jnp.zeros((heads, length), jnp.float32),
        jnp.zeros((length, heads, HD), jnp.float32),
    )
    key_piece = lax.all_gather(key_rows, "span", axis=0, tiled=True)
    value_piece = lax.all_gather(value_rows, "span", axis=0, tiled=True)
    count = key_piece.shape[0]
    block = math.gcd(count, 512)

    def one_block(index, state):
        top, total, accum = state
        offset = index * block
        key_block = lax.dynamic_slice_in_dim(key_piece, offset, block, 0).reshape(block, heads, HD)
        value_block = lax.dynamic_slice_in_dim(value_piece, offset, block, 0).reshape(
            block, heads, HD
        )
        scores = (
            jnp.einsum("qhd,khd->hqk", query_three, key_block, preferred_element_type=jnp.float32)
            * scale
        )
        keep = offset + jnp.arange(block) < limit
        scores = jnp.where(keep[None, None, :], scores, masked_score)
        new_top = jnp.maximum(top, jnp.max(scores, axis=-1))
        expo = jnp.where(keep[None, None, :], jnp.exp(scores - new_top[:, :, None]), 0.0)
        shrink = jnp.exp(top - new_top)
        total = total * shrink + jnp.sum(expo, axis=-1)
        mixed = jnp.einsum(
            "hqk,khd->qhd",
            expo.astype(jnp.bfloat16),
            value_block,
            preferred_element_type=jnp.float32,
        )
        accum = accum * shrink.T[:, :, None] + mixed
        return (new_top, total, accum)

    def run_blocks(state):
        return lax.fori_loop(0, count // block, one_block, state)

    def keep_state(state):
        return state

    top, total, accum = lax.cond(jnp.int32(0) < limit, run_blocks, keep_state, init)
    attn = (accum / total.T[:, :, None]).reshape(length, columns).astype(jnp.bfloat16)
    token_rows = lax.all_to_all(attn, "seq", split_axis=0, concat_axis=1, tiled=True)
    steps_count = gate_table.shape[0]
    span_step = lax.dynamic_index_in_dim(timesteps, span_id, 0, keepdims=False)
    picked = (jnp.arange(steps_count) == span_step).astype(jnp.float32)
    gate = jnp.dot(picked, gate_table, precision=lax.Precision.HIGHEST)
    return (token_rows.astype(jnp.float32) * gate[None, :]).astype(jnp.bfloat16)[None]


def solution(mesh):
    in_specs = (
        P(("parts", "span"), "seq", None),
        P(("parts", "span"), "seq", None),
        P(("parts", "span"), "seq", None),
        P("parts"),
        P(),
    )
    out_specs = P(("parts", "span"), "seq", None)
    return jax.shard_map(local, mesh=mesh, in_specs=in_specs, out_specs=out_specs, check_vma=False)
```

profile of v0, /device:TPU:0, one launch (start us, length us, event | category | flops | bytes accessed | tf_op | source)
XLA Modules:
  0.0 533.7 jit_solution(13859830746761117424)
XLA Ops:
  6.5 4.1 copy.30
  10.7 54.5 %all_to_all.64 = bf16[256,4,1024]{0,2,1:T(8,128)(2,1)S(1)} all-to-all(bf16[256,4,1024]{0,2,1:T(8,128)(2,1)} %bitcast.80), channel_id=1, replica_groups=mesh['parts'=2,'span'=4,'seq'=4] {'seq'}, dimensions={1} | all-to-all | bytes 4194304 | tf_op jit(solution)/shard_map/all_to_all | solution.py:14
  65.2 2.5 copy.31
  67.7 4.1 copy.32
  71.8 51.0 %all_to_all.65 = bf16[256,4,1024]{0,2,1:T(8,128)(2,1)S(1)} all-to-all(bf16[256,4,1024]{0,2,1:T(8,128)(2,1)} %bitcast.81), channel_id=1, replica_groups=mesh['parts'=2,'span'=4,'seq'=4] {'seq'}, dimensions={1} | all-to-all | bytes 4194304 | tf_op jit(solution)/shard_map/all_to_all | solution.py:15
  122.8 2.4 copy.33
  125.2 4.1 copy.29
  129.3 3.6 all-to-all-start
  132.9 47.3 %all-to-all-done = bf16[256,4,1024]{0,2,1:T(8,128)(2,1)S(1)} async-done(((bf16[256,4,1024]{0,2,1:T(8,128)(2,1)}), bf16[256,4,1024]{0,2,1:T(8,128)(2,1)S(1)}, u32[]{:S(2)}, u32[]{:S(2)}) %all-to-all-start) | async-done | bytes 2097184 | tf_op jit(solution)/shard_map/all_to_all | solution.py:13
  180.2 5.0 all-gather.5.cloned.1.call-done
  185.2 271.6 %conditional.1 = (f32[8,1024]{1,0:T(8,128)}, f32[1024,8,128]{0,2,1:T(8,128)}) conditional(s32[]{:T(128)} %convert_element_type.44, () %tuple.27, (bf16[4,256,1024]{1,2,0:T(8,128)(2,1)S(1)}, s32[]{:T(128)}, bf16[4096,1024]{1,0:T(8,128)(2,1)}, bf16[4096,1024]{1,0:T(8,128)(2,1)}) %tuple.65), branch_computations={%region_0.0_spmd, %region_1.6_spmd} | conditional | flops 2205205504 | bytes 151521616 | solution.py:66
  185.2 2.4 copy.34
  187.6 2.2 copy.45
  189.8 1.7 copy.28
  191.5 265.3 %while.17 = (s32[]{:T(128)}, f32[8,1024]{1,0:T(8,128)S(1)}, f32[8,1024]{1,0:T(8,128)}, f32[1024,8,128]{0,2,1:T(8,128)}, s32[]{:T(128)}, /*index=5*/bf16[4096,102...) while((s32[]{:T(128)}, f32[8,1024]{1,0:T(8,128)S(1)}, ...), condition=%wide.region_5.5_spmd.clone, body=%wide.region_2.4_spmd.clone.sunk | while | flops 2205205504 | bytes 138938576 | solution.py:61
  191.5 2.7 constant_dynamic-slice_fusion.3
  194.2 1.5 copy.48
  195.7 9.4 %bitcast_reduce_fusion.2 = (f32[8,1024]{1,0:T(8,128)S(1)}, f32[8,512,1024]{2,1,0:T(8,128)}) fusion(pred[512]{0:T(512)(128)(4,1)S(1)} %add_compare_fusion.2, bf16[512,8,128]{0,2,1:T(8,128)(2,1)S(1)} %bitcast.72, bf16[1024,8,128]{2,0,1:T(8,128)(2,1)} %get-tuple-element.338), kind=kOutput, calls=%fused_computation.1.clone.1 | convolution fusion | flops 1086316544 | bytes 19956224 | tf_op jit(solution)/shard_map/cond/branch_1_fun/while/body/eval_jaxpr/qhd,khd->hqk/dot_general | solution.py:42
  205.6 10.9 %bitcast_add_fusion.2 = f32[1024,8,128]{0,2,1:T(8,128)} fusion(f32[1024,8,128]{0,2,1:T(8,128)} %get-tuple-element.323, bf16[512,8,128]{0,2,1:T(8,128)(2,1)S(1)} %bitcast.73, f32[8,512,1024]{2,1,0:T(8,128)} %get-tuple-element.305, f32[8,1024]{1,0:T(8,128)S(1)} %get-tuple-element.333, pred[512]{0:T(512)(128)(4,1)S(1)} %add_compare_fusion.2, ...), kind=kOutput, calls=%fused_computation.10.clone.1 | convolution fusion | flops 1097859072 | bytes 26280448 | tf_op jit(solution)/shard_map/cond/branch_1_fun/while/body/eval_jaxpr/hqk,khd->qhd/dot_general | solution.py:51
  217.7 4.6 fusion.37
  222.9 2.7 constant_dynamic-slice_fusion.3
  225.6 1.5 copy.48
  227.1 9.4 %bitcast_reduce_fusion.2 = (f32[8,1024]{1,0:T(8,128)S(1)}, f32[8,512,1024]{2,1,0:T(8,128)}) fusion(pred[512]{0:T(512)(128)(4,1)S(1)} %add_compare_fusion.2, bf16[512,8,128]{0,2,1:T(8,128)(2,1)S(1)} %bitcast.72, bf16[1024,8,128]{2,0,1:T(8,128)(2,1)} %get-tuple-element.338), kind=kOutput, calls=%fused_computation.1.clone.1 | convolution fusion | flops 1086316544 | bytes 19956224 | tf_op jit(solution)/shard_map/cond/branch_1_fun/while/body/eval_jaxpr/qhd,khd->hqk/dot_general | solution.py:42
  237.1 12.1 %bitcast_add_fusion.2 = f32[1024,8,128]{0,2,1:T(8,128)} fusion(f32[1024,8,128]{0,2,1:T(8,128)} %get-tuple-element.323, bf16[512,8,128]{0,2,1:T(8,128)(2,1)S(1)} %bitcast.73, f32[8,512,1024]{2,1,0:T(8,128)} %get-tuple-element.305, f32[8,1024]{1,0:T(8,128)S(1)} %get-tuple-element.333, pred[512]{0:T(512)(128)(4,1)S(1)} %add_compare_fusion.2, ...), kind=kOutput, calls=%fused_computation.10.clone.1 | convolution fusion | flops 1097859072 | bytes 26280448 | tf_op jit(solution)/shard_map/cond/branch_1_fun/while/body/eval_jaxpr/hqk,khd->qhd/dot_general | solution.py:51
  250.3 4.6 fusion.37
  256.3 2.7 constant_dynamic-slice_fusion.3
  259.0 1.5 copy.48
  260.5 9.4 %bitcast_reduce_fusion.2 = (f32[8,1024]{1,0:T(8,128)S(1)}, f32[8,512,1024]{2,1,0:T(8,128)}) fusion(pred[512]{0:T(512)(128)(4,1)S(1)} %add_compare_fusion.2, bf16[512,8,128]{0,2,1:T(8,128)(2,1)S(1)} %bitcast.72, bf16[1024,8,128]{2,0,1:T(8,128)(2,1)} %get-tuple-element.338), kind=kOutput, calls=%fused_computation.1.clone.1 | convolution fusion | flops 1086316544 | bytes 19956224 | tf_op jit(solution)/shard_map/cond/branch_1_fun/while/body/eval_jaxpr/qhd,khd->hqk/dot_general | solution.py:42
  270.5 12.1 %bitcast_add_fusion.2 = f32[1024,8,128]{0,2,1:T(8,128)} fusion(f32[1024,8,128]{0,2,1:T(8,128)} %get-tuple-element.323, bf16[512,8,128]{0,2,1:T(8,128)(2,1)S(1)} %bitcast.73, f32[8,512,1024]{2,1,0:T(8,128)} %get-tuple-element.305, f32[8,1024]{1,0:T(8,128)S(1)} %get-tuple-element.333, pred[512]{0:T(512)(128)(4,1)S(1)} %add_compare_fusion.2, ...), kind=kOutput, calls=%fused_computation.10.clone.1 | convolution fusion | flops 1097859072 | bytes 26280448 | tf_op jit(solution)/shard_map/cond/branch_1_fun/while/body/eval_jaxpr/hqk,khd->qhd/dot_general | solution.py:51
  283.7 4.6 fusion.37
  288.4 1.4 fusion.38
  289.8 2.7 constant_dynamic-slice_fusion.3
  292.4 1.5 copy.48
  293.9 9.4 %bitcast_reduce_fusion.2 = (f32[8,1024]{1,0:T(8,128)S(1)}, f32[8,512,1024]{2,1,0:T(8,128)}) fusion(pred[512]{0:T(512)(128)(4,1)S(1)} %add_compare_fusion.2, bf16[512,8,128]{0,2,1:T(8,128)(2,1)S(1)} %bitcast.72, bf16[1024,8,128]{2,0,1:T(8,128)(2,1)} %get-tuple-element.338), kind=kOutput, calls=%fused_computation.1.clone.1 | convolution fusion | flops 1086316544 | bytes 19956224 | tf_op jit(solution)/shard_map/cond/branch_1_fun/while/body/eval_jaxpr/qhd,khd->hqk/dot_general | solution.py:42
  303.9 12.1 %bitcast_add_fusion.2 = f32[1024,8,128]{0,2,1:T(8,128)} fusion(f32[1024,8,128]{0,2,1:T(8,128)} %get-tuple-element.323, bf16[512,8,128]{0,2,1:T(8,128)(2,1)S(1)} %bitcast.73, f32[8,512,1024]{2,1,0:T(8,128)} %get-tuple-element.305, f32[8,1024]{1,0:T(8,128)S(1)} %get-tuple-element.333, pred[512]{0:T(512)(128)(4,1)S(1)} %add_compare_fusion.2, ...), kind=kOutput, calls=%fused_computation.10.clone.1 | convolution fusion | flops 1097859072 | bytes 26280448 | tf_op jit(solution)/shard_map/cond/branch_1_fun/while/body/eval_jaxpr/hqk,khd->qhd/dot_general | solution.py:51
  317.1 4.6 fusion.37
  321.8 1.4 fusion.38
  323.2 2.7 constant_dynamic-slice_fusion.3
  325.8 1.5 copy.48
  327.4 9.4 %bitcast_reduce_fusion.2 = (f32[8,1024]{1,0:T(8,128)S(1)}, f32[8,512,1024]{2,1,0:T(8,128)}) fusion(pred[512]{0:T(512)(128)(4,1)S(1)} %add_compare_fusion.2, bf16[512,8,128]{0,2,1:T(8,128)(2,1)S(1)} %bitcast.72, bf16[1024,8,128]{2,0,1:T(8,128)(2,1)} %get-tuple-element.338), kind=kOutput, calls=%fused_computation.1.clone.1 | convolution fusion | flops 1086316544 | bytes 19956224 | tf_op jit(solution)/shard_map/cond/branch_1_fun/while/body/eval_jaxpr/qhd,khd->hqk/dot_general | solution.py:42
  337.3 12.1 %bitcast_add_fusion.2 = f32[1024,8,128]{0,2,1:T(8,128)} fusion(f32[1024,8,128]{0,2,1:T(8,128)} %get-tuple-element.323, bf16[512,8,128]{0,2,1:T(8,128)(2,1)S(1)} %bitcast.73, f32[8,512,1024]{2,1,0:T(8,128)} %get-tuple-element.305, f32[8,1024]{1,0:T(8,128)S(1)} %get-tuple-element.333, pred[512]{0:T(512)(128)(4,1)S(1)} %add_compare_fusion.2, ...), kind=kOutput, calls=%fused_computation.10.clone.1 | convolution fusion | flops 1097859072 | bytes 26280448 | tf_op jit(solution)/shard_map/cond/branch_1_fun/while/body/eval_jaxpr/hqk,khd->qhd/dot_general | solution.py:51
  350.5 4.6 fusion.37
  356.6 2.7 constant_dynamic-slice_fusion.3
  359.3 1.5 copy.48
  360.8 9.4 %bitcast_reduce_fusion.2 = (f32[8,1024]{1,0:T(8,128)S(1)}, f32[8,512,1024]{2,1,0:T(8,128)}) fusion(pred[512]{0:T(512)(128)(4,1)S(1)} %add_compare_fusion.2, bf16[512,8,128]{0,2,1:T(8,128)(2,1)S(1)} %bitcast.72, bf16[1024,8,128]{2,0,1:T(8,128)(2,1)} %get-tuple-element.338), kind=kOutput, calls=%fused_computation.1.clone.1 | convolution fusion | flops 1086316544 | bytes 19956224 | tf_op jit(solution)/shard_map/cond/branch_1_fun/while/body/eval_jaxpr/qhd,khd->hqk/dot_general | solution.py:42
  370.7 12.1 %bitcast_add_fusion.2 = f32[1024,8,128]{0,2,1:T(8,128)} fusion(f32[1024,8,128]{0,2,1:T(8,128)} %get-tuple-element.323, bf16[512,8,128]{0,2,1:T(8,128)(2,1)S(1)} %bitcast.73, f32[8,512,1024]{2,1,0:T(8,128)} %get-tuple-element.305, f32[8,1024]{1,0:T(8,128)S(1)} %get-tuple-element.333, pred[512]{0:T(512)(128)(4,1)S(1)} %add_compare_fusion.2, ...), kind=kOutput, calls=%fused_computation.10.clone.1 | convolution fusion | flops 1097859072 | bytes 26280448 | tf_op jit(solution)/shard_map/cond/branch_1_fun/while/body/eval_jaxpr/hqk,khd->qhd/dot_general | solution.py:51
  383.9 4.6 fusion.37
  390.0 2.7 constant_dynamic-slice_fusion.3
  392.7 1.5 copy.48
  394.2 9.4 %bitcast_reduce_fusion.2 = (f32[8,1024]{1,0:T(8,128)S(1)}, f32[8,512,1024]{2,1,0:T(8,128)}) fusion(pred[512]{0:T(512)(128)(4,1)S(1)} %add_compare_fusion.2, bf16[512,8,128]{0,2,1:T(8,128)(2,1)S(1)} %bitcast.72, bf16[1024,8,128]{2,0,1:T(8,128)(2,1)} %get-tuple-element.338), kind=kOutput, calls=%fused_computation.1.clone.1 | convolution fusion | flops 1086316544 | bytes 19956224 | tf_op jit(solution)/shard_map/cond/branch_1_fun/while/body/eval_jaxpr/qhd,khd->hqk/dot_general | solution.py:42
  404.1 12.1 %bitcast_add_fusion.2 = f32[1024,8,128]{0,2,1:T(8,128)} fusion(f32[1024,8,128]{0,2,1:T(8,128)} %get-tuple-element.323, bf16[512,8,128]{0,2,1:T(8,128)(2,1)S(1)} %bitcast.73, f32[8,512,1024]{2,1,0:T(8,128)} %get-tuple-element.305, f32[8,1024]{1,0:T(8,128)S(1)} %get-tuple-element.333, pred[512]{0:T(512)(128)(4,1)S(1)} %add_compare_fusion.2, ...), kind=kOutput, calls=%fused_computation.10.clone.1 | convolution fusion | flops 1097859072 | bytes 26280448 | tf_op jit(solution)/shard_map/cond/branch_1_fun/while/body/eval_jaxpr/hqk,khd->qhd/dot_general | solution.py:51
  417.4 4.6 fusion.37
  423.4 2.7 constant_dynamic-slice_fusion.3
  426.1 1.5 copy.48
  427.6 9.4 %bitcast_reduce_fusion.2 = (f32[8,1024]{1,0:T(8,128)S(1)}, f32[8,512,1024]{2,1,0:T(8,128)}) fusion(pred[512]{0:T(512)(128)(4,1)S(1)} %add_compare_fusion.2, bf16[512,8,128]{0,2,1:T(8,128)(2,1)S(1)} %bitcast.72, bf16[1024,8,128]{2,0,1:T(8,128)(2,1)} %get-tuple-element.338), kind=kOutput, calls=%fused_computation.1.clone.1 | convolution fusion | flops 1086316544 | bytes 19956224 | tf_op jit(solution)/shard_map/cond/branch_1_fun/while/body/eval_jaxpr/qhd,khd->hqk/dot_general | solution.py:42
  437.5 12.1 %bitcast_add_fusion.2 = f32[1024,8,128]{0,2,1:T(8,128)} fusion(f32[1024,8,128]{0,2,1:T(8,128)} %get-tuple-element.323, bf16[512,8,128]{0,2,1:T(8,128)(2,1)S(1)} %bitcast.73, f32[8,512,1024]{2,1,0:T(8,128)} %get-tuple-element.305, f32[8,1024]{1,0:T(8,128)S(1)} %get-tuple-element.333, pred[512]{0:T(512)(128)(4,1)S(1)} %add_compare_fusion.2, ...), kind=kOutput, calls=%fused_computation.10.clone.1 | convolution fusion | flops 1097859072 | bytes 26280448 | tf_op jit(solution)/shard_map/cond/branch_1_fun/while/body/eval_jaxpr/hqk,khd->qhd/dot_general | solution.py:51
  450.8 4.6 fusion.37
  456.8 2.8 divide_convert_fusion
  459.6 2.8 reshape.90
  462.4 4.3 copy.42
  466.7 4.6 all-to-all-start.3
  472.8 47.3 %all-to-all-done.3 = bf16[4,256,1024]{2,1,0:T(8,128)(2,1)} async-done(((bf16[4,256,1024]{2,1,0:T(8,128)(2,1)}), bf16[4,256,1024]{2,1,0:T(8,128)(2,1)}, u32[]{:S(2)}, u32[]{:S(2)}) %all-to-all-start.3) | async-done | bytes 2097184 | tf_op jit(solution)/shard_map/all_to_all | solution.py:68
  520.1 2.8 copy.38
  524.0 2.9 copy.39
  (70 shorter events, 24.3 us)
Async XLA Ops:
  6.5 465.3 %copy-start = (f32[32,4096]{1,0:T(8,128)S(1)}, f32[32,4096]{1,0:T(8,128)}, u32[]{:S(2)}) copy-start(f32[32,4096]{1,0:T(8,128)} %param.13) | copy-start | bytes 1572868
  6.5 173.7 %all-gather.3.cloned.1.call-start = ((), (), s32[]{:S(2)}) async-start(), calls=%async_computation.4 | async-start | bytes 10485760 | tf_op jit(solution)/shard_map/all_gather | solution.py:29
  67.7 117.5 %all-gather.5.cloned.1.call-start = ((), (), s32[]{:S(2)}) async-start(), calls=%async_computation.5 | async-start | bytes 10485760 | tf_op jit(solution)/shard_map/all_gather | solution.py:30
  129.3 50.9 %all-to-all-start = ((bf16[256,4,1024]{0,2,1:T(8,128)(2,1)}), bf16[256,4,1024]{0,2,1:T(8,128)(2,1)S(1)}, u32[]{:S(2)}, u32[]{:S(2)}) async-start(bf16[256,4,1024]{0,2,1:T(8,128)(2,1)} %bitcast.78), calls=%async_computation | async-start | bytes 4194304 | tf_op jit(solution)/shard_map/all_to_all | solution.py:13
  205.6 12.1 %copy-start.1 = (f32[8,512,1024]{2,1,0:T(8,128)S(1)}, f32[8,512,1024]{2,1,0:T(8,128)}, u32[]{:S(2)}) copy-start(f32[8,512,1024]{2,1,0:T(8,128)} %get-tuple-element.305) | copy-start | bytes 50331652 | tf_op jit(solution)/shard_map/cond/branch_1_fun/while
  237.1 13.3 %copy-start.1 = (f32[8,512,1024]{2,1,0:T(8,128)S(1)}, f32[8,512,1024]{2,1,0:T(8,128)}, u32[]{:S(2)}) copy-start(f32[8,512,1024]{2,1,0:T(8,128)} %get-tuple-element.305) | copy-start | bytes 50331652 | tf_op jit(solution)/shard_map/cond/branch_1_fun/while
  270.5 13.3 %copy-start.1 = (f32[8,512,1024]{2,1,0:T(8,128)S(1)}, f32[8,512,1024]{2,1,0:T(8,128)}, u32[]{:S(2)}) copy-start(f32[8,512,1024]{2,1,0:T(8,128)} %get-tuple-element.305) | copy-start | bytes 50331652 | tf_op jit(solution)/shard_map/cond/branch_1_fun/while
  303.9 13.3 %copy-start.1 = (f32[8,512,1024]{2,1,0:T(8,128)S(1)}, f32[8,512,1024]{2,1,0:T(8,128)}, u32[]{:S(2)}) copy-start(f32[8,512,1024]{2,1,0:T(8,128)} %get-tuple-element.305) | copy-start | bytes 50331652 | tf_op jit(solution)/shard_map/cond/branch_1_fun/while
  337.3 13.3 %copy-start.1 = (f32[8,512,1024]{2,1,0:T(8,128)S(1)}, f32[8,512,1024]{2,1,0:T(8,128)}, u32[]{:S(2)}) copy-start(f32[8,512,1024]{2,1,0:T(8,128)} %get-tuple-element.305) | copy-start | bytes 50331652 | tf_op jit(solution)/shard_map/cond/branch_1_fun/while
  370.7 13.3 %copy-start.1 = (f32[8,512,1024]{2,1,0:T(8,128)S(1)}, f32[8,512,1024]{2,1,0:T(8,128)}, u32[]{:S(2)}) copy-start(f32[8,512,1024]{2,1,0:T(8,128)} %get-tuple-element.305) | copy-start | bytes 50331652 | tf_op jit(solution)/shard_map/cond/branch_1_fun/while
  404.1 13.3 %copy-start.1 = (f32[8,512,1024]{2,1,0:T(8,128)S(1)}, f32[8,512,1024]{2,1,0:T(8,128)}, u32[]{:S(2)}) copy-start(f32[8,512,1024]{2,1,0:T(8,128)} %get-tuple-element.305) | copy-start | bytes 50331652 | tf_op jit(solution)/shard_map/cond/branch_1_fun/while
  437.5 13.3 %copy-start.1 = (f32[8,512,1024]{2,1,0:T(8,128)S(1)}, f32[8,512,1024]{2,1,0:T(8,128)}, u32[]{:S(2)}) copy-start(f32[8,512,1024]{2,1,0:T(8,128)} %get-tuple-element.305) | copy-start | bytes 50331652 | tf_op jit(solution)/shard_map/cond/branch_1_fun/while
  462.4 8.9 %copy-start.2 = (s32[4]{0:T(128)S(1)}, s32[4]{0:T(128)}, u32[]{:S(2)}) copy-start(s32[4]{0:T(128)} %param.12) | copy-start | bytes 52
  466.7 53.4 %all-to-all-start.3 = ((bf16[4,256,1024]{2,1,0:T(8,128)(2,1)}), bf16[4,256,1024]{2,1,0:T(8,128)(2,1)}, u32[]{:S(2)}, u32[]{:S(2)}) async-start(bf16[4,256,1024]{2,1,0:T(8,128)(2,1)} %copy.42), calls=%async_computation.3 | async-start | bytes 4194304 | tf_op jit(solution)/shard_map/all_to_all | solution.py:68
Sparse Core Ops, SparseCore 0:
  67.8 57.4 all-gather.2
  126.9 58.2 all-gather.4
where the time goes:
time: 536 us; the launch traced here: 534 us
  matrix products  171 us (32%)
  blocking collectives  105 us (20%)
  waiting for transfers between devices  99.6 us (19%)
  local copies, waits for them, and re-layouts  84 us (16%)
  other arithmetic  51.5 us (10%)
  between operations  13.5 us (3%)
  starting transfers between devices  8.25 us (2%)
    dot_general x8, matrix products, one_block(): jnp.einsum('hqk,khd->qhd', expo.astype(jnp.bfloat16), value_block, prefer...  95.3 us
    dot_general x8, matrix products, one_block(): jnp.einsum('qhd,khd->hqk', query_three, key_block, preferred_element_type...  74.9 us
    all_to_all x1, blocking collectives, local(): lax.all_to_all(k_in[0], 'seq', split_axis=1, concat_axis=0, tiled=True)  54.5 us
    all_to_all x1, blocking collectives, local(): lax.all_to_all(v_in[0], 'seq', split_axis=1, concat_axis=0, tiled=True)  51 us
    all_to_all x1, waiting for transfers between devices, local(): lax.all_to_all(q_in[0], 'seq', split_axis=1, concat_axis=0, tiled=True)  47.3 us
    all_to_all x1, waiting for transfers between devices, local(): lax.all_to_all(attn, 'seq', split_axis=0, concat_axis=1, tiled=True)  47.3 us
    reduce_sum x8, other arithmetic, one_block(): total = total * shrink + jnp.sum(expo, axis=-1)  37 us
    dynamic_slice x16, local copies, waits for them, and re-layouts, one_block(): lax.dynamic_slice_in_dim(value_piece, offset, block, 0)  25.8 us
  transfers between devices with their start and end apart: 4, of which 3 were waited for; matrix products, arithmetic and copies ran while one was open for 2% of the time, Pallas kernels for 0%

commit v1 on v0

--- a/solution.py
+++ b/solution.py
@@ -1,18 +1,51 @@
+import functools
 import math
 import jax
 import jax.numpy as jnp
 from jax import lax
 from jax.sharding import PartitionSpec as P
+from jax.lax import axis_index, axis_size, ppermute
 
 HD = 128
 masked_score = -1e30
+
+
+def goods_hold(vals, dim_at, field):
+    prior, inter = (vals.shape[:dim_at], vals.shape[dim_at + 1 :])
+    return jnp.moveaxis(vals.reshape(*prior, field, -1, *inter), dim_at, 0)
+
+
+def watch_the_cards(v0, on_dim):
+    v0 = jnp.moveaxis(v0, 0, on_dim)
+    field_out = v0.shape
+    return v0.reshape(
+        *field_out[:on_dim], field_out[on_dim] * field_out[on_dim + 1], *field_out[on_dim + 2 :]
+    )
+
+
+def expand_the_targets(here_x, device_axis, point, x0):
+    aux = axis_size(device_axis)
+    a_now = axis_index(device_axis)
+    odd, low = (aux, a_now)
+    taken_in = goods_hold(here_x, point, odd)
+    parts_seen = [taken_in[low]]
+    for w in range(1, odd):
+        found_now = taken_in[low ^ w]
+        parts_seen.append(
+            ppermute(found_now, device_axis, [(to_i, to_i ^ w) for to_i in range(odd)])
+        )
+    taken_in = jnp.stack(parts_seen)[low ^ jnp.arange(odd)]
+    return watch_the_cards(taken_in, x0)
+
+
+report_the_terms = functools.partial(expand_the_targets, device_axis="seq", point=1, x0=0)
 
 
 def local(q_in, k_in, v_in, timesteps, gate_table):
     head_rows, key_rows, value_rows = (
         lax.all_to_all(q_in[0], "seq", split_axis=1, concat_axis=0, tiled=True),
         lax.all_to_all(k_in[0], "seq", split_axis=1, concat_axis=0, tiled=True),
-        lax.all_to_all(v_in[0], "seq", split_axis=1, concat_axis=0, tiled=True),
+        report_the_terms(v_in[0]),
     )
     length = head_rows.shape[0]
     columns = head_rows.shape[1]

time: 536 us -> 519 us (0.968)
  blocking collectives: 105 us -> 59.6 us
  waiting for transfers between devices: 99.6 us -> 134 us
  local copies, waits for them, and re-layouts: 84 us -> 70.4 us
  starting transfers between devices: 8.25 us -> 14.3 us
    all_to_all x1 -> x0, blocking collectives: 51 us -> none  [local(): lax.all_to_all(v_in[0], 'seq', split_axis=1, concat_axis=0, tiled=True)]
    ppermute x0 -> x3, waiting for transfers between devices: none -> 33.2 us  [expand_the_targets(): ppermute(found_now, device_axis, [(to_i, to_i ^ w) for to_i in range(odd)])]
    dynamic_slice x16 -> x8, local copies, waits for them, and re-layouts: 25.8 us -> 11.6 us  [one_block(): lax.dynamic_slice_in_dim(value_piece, offset, block, 0)]
    while x24 -> x72, local copies, waits for them, and re-layouts: 9.48 us -> 0.18 us
    all_gather x1, waiting for transfers between devices: 0.01 us -> 6 us  [local(): key_piece = lax.all_gather(key_rows, 'span', axis=0, tiled=True)]
    another operation x1 -> x6, local copies, waits for them, and re-layouts: 2.36 us -> 8.3 us
    ppermute x0 -> x3, starting transfers between devices: none -> 5.82 us  [expand_the_targets(): ppermute(found_now, device_axis, [(to_i, to_i ^ w) for to_i in range(odd)])]
    dynamic_slice x8 -> x16, local copies, waits for them, and re-layouts: 11.9 us -> 14.7 us  [one_block(): lax.dynamic_slice_in_dim(key_piece, offset, block, 0)]
  transfers between devices with their start and end apart: 4 -> 7, of which waited for: 3 -> 5; matrix products, arithmetic and copies ran while one was open for 2% -> 3% of each run, Pallas kernels for 0% -> 0%
where the time goes in v1:
time: 519 us; the launch traced here: 517 us
  matrix products  172 us (33%)
  waiting for transfers between devices  134 us (26%)
  local copies, waits for them, and re-layouts  70.4 us (14%)
  blocking collectives  59.6 us (11%)
  other arithmetic  53.3 us (10%)
  starting transfers between devices  14.3 us (3%)
  between operations  13.5 us (3%)
    dot_general x8, matrix products, one_block(): jnp.einsum('hqk,khd->qhd', expo.astype(jnp.bfloat16), value_block, prefer...  95.2 us
    dot_general x8, matrix products, one_block(): jnp.einsum('qhd,khd->hqk', query_three, key_block, preferred_element_type...  75.4 us
    all_to_all x1, blocking collectives, local(): lax.all_to_all(k_in[0], 'seq', split_axis=1, concat_axis=0, tiled=True)  59.6 us
    all_to_all x1, waiting for transfers between devices, local(): lax.all_to_all(q_in[0], 'seq', split_axis=1, concat_axis=0, tiled=True)  47.5 us
    all_to_all x1, waiting for transfers between devices, local(): lax.all_to_all(attn, 'seq', split_axis=0, concat_axis=1, tiled=True)  47.3 us
    reduce_sum x8, other arithmetic, one_block(): total = total * shrink + jnp.sum(expo, axis=-1)  37.1 us
    ppermute x3, waiting for transfers between devices, expand_the_targets(): ppermute(found_now, device_axis, [(to_i, to_i ^ w) for to_i in range(odd)])  33.2 us
    dynamic_slice x16, local copies, waits for them, and re-layouts, one_block(): lax.dynamic_slice_in_dim(key_piece, offset, block, 0)  14.7 us
  transfers between devices with their start and end apart: 7, of which 5 were waited for; matrix products, arithmetic and copies ran while one was open for 3% of the time, Pallas kernels for 0%

profile of v1, /device:TPU:0, one launch (start us, length us, event | category | flops | bytes accessed | tf_op | source)
XLA Modules:
  0.0 517.3 jit_solution(12024312783753112834)
XLA Ops:
  6.5 3.3 copy.49
  12.3 4.1 collective-permute-start.1
  17.7 1.4 collective-permute-start.2
  21.7 30.0 %collective-permute-done.1 = bf16[256,1024]{1,0:T(8,128)(2,1)S(1)} collective-permute-done((bf16[256,1024]{1,0:T(8,128)(2,1)S(1)}, bf16[256,1024]{1,0:T(8,128)(2,1)S(1)}, u32[]{:S(2)}, u32[]{:S(2)}) %collective-permute-start.1) | collective-permute-done | bytes 524320 | tf_op jit(solution)/shard_map/ppermute | solution.py:35
  51.7 3.2 collective-permute-done
  54.9 1.8 pad_maximum_fusion
  56.7 2.0 gather_fusion
  58.7 4.1 copy.54
  62.9 2.5 copy.47
  65.3 59.6 %all_to_all.45 = bf16[256,4,1024]{0,2,1:T(8,128)(2,1)S(1)} all-to-all(bf16[256,4,1024]{0,2,1:T(8,128)(2,1)} %bitcast.90), channel_id=1, replica_groups=mesh['parts'=2,'span'=4,'seq'=4] {'seq'}, dimensions={1} | all-to-all | bytes 4194304 | tf_op jit(solution)/shard_map/all_to_all | solution.py:47
  124.9 2.4 copy.48
  127.3 4.1 copy.46
  131.5 3.8 all-to-all-start
  135.3 47.5 %all-to-all-done = bf16[256,4,1024]{0,2,1:T(8,128)(2,1)S(1)} async-done(((bf16[256,4,1024]{0,2,1:T(8,128)(2,1)}), bf16[256,4,1024]{0,2,1:T(8,128)(2,1)S(1)}, u32[]{:S(2)}, u32[]{:S(2)}) %all-to-all-start) | async-done | bytes 2097184 | tf_op jit(solution)/shard_map/all_to_all | solution.py:46
  182.7 6.0 %all-gather.3.cloned.1.call-done = bf16[4096,1024]{1,0:T(8,128)(2,1)} async-done(((bf16[1024,1024]{1,0:T(8,128)(2,1)}), bf16[4096,1024]{1,0:T(8,128)(2,1)}) %all-gather.3.cloned.1.call-update) | async-done | bytes 8388624 | tf_op jit(solution)/shard_map/all_gather | solution.py:62
  188.7 251.7 %conditional.1 = (f32[8,1024]{1,0:T(8,128)}, f32[1024,8,128]{0,2,1:T(8,128)}) conditional(s32[]{:T(128)} %convert_element_type.44, () %tuple.27, (bf16[4,256,1024]{1,2,0:T(8,128)(2,1)S(1)}, s32[]{:T(128)}, bf16[4096,1024]{1,0:T(8,128)(2,1)}, bf16[4096,1024]{0,1:T(8,128)(2,1)}) %tuple.67), branch_computations={%region_0.0_spmd, %region_1.6_spmd} | conditional | flops 2205205504 | bytes 132647312 | solution.py:99
  188.7 2.4 copy.55
  191.1 2.2 copy.64
  193.3 1.7 copy.45
  195.0 245.4 %while.17 = (s32[]{:T(128)}, f32[8,1024]{1,0:T(8,128)S(1)}, f32[8,1024]{1,0:T(8,128)}, f32[1024,8,128]{0,2,1:T(8,128)}, s32[]{:T(128)}, /*index=5*/bf16[4096,102...) while((s32[]{:T(128)}, f32[8,1024]{1,0:T(8,128)S(1)}, ...), condition=%wide.region_5.5_spmd.clone, body=%wide.region_2.4_spmd.clone.sunk | while | flops 2205205504 | bytes 120064280 | solution.py:94
  196.8 9.4 %bitcast_reduce_fusion.2 = (f32[8,1024]{1,0:T(8,128)S(1)}, f32[8,512,1024]{2,1,0:T(8,128)}) fusion(pred[512]{0:T(512)(128)(4,1)S(1)} %add_compare_fusion.2, bf16[512,8,128]{0,2,1:T(8,128)(2,1)S(1)} %bitcast.81, bf16[1024,8,128]{2,0,1:T(8,128)(2,1)} %get-tuple-element.348), kind=kOutput, calls=%fused_computation.2.clone.1 | convolution fusion | flops 1086316544 | bytes 19956224 | tf_op jit(solution)/shard_map/cond/branch_1_fun/while/body/eval_jaxpr/qhd,khd->hqk/dot_general | solution.py:75
  206.3 1.5 constant_dynamic-slice_fusion.9
  207.8 10.9 %bitcast_add_fusion.2 = f32[1024,8,128]{0,2,1:T(8,128)} fusion(f32[1024,8,128]{0,2,1:T(8,128)} %get-tuple-element.333, bf16[512,8,128]{0,2,1:T(8,128)(2,1)S(1)} %bitcast.82, f32[8,512,1024]{2,1,0:T(8,128)} %get-tuple-element.316, f32[8,1024]{1,0:T(8,128)S(1)} %get-tuple-element.343, pred[512]{0:T(512)(128)(4,1)S(1)} %add_compare_fusion.2, ...), kind=kOutput, calls=%fused_computation.11.clone.1 | convolution fusion | flops 1097859072 | bytes 26280448 | tf_op jit(solution)/shard_map/cond/branch_1_fun/while/body/eval_jaxpr/hqk,khd->qhd/dot_general | solution.py:84
  218.7 4.6 fusion.38
  225.8 9.4 %bitcast_reduce_fusion.2 = (f32[8,1024]{1,0:T(8,128)S(1)}, f32[8,512,1024]{2,1,0:T(8,128)}) fusion(pred[512]{0:T(512)(128)(4,1)S(1)} %add_compare_fusion.2, bf16[512,8,128]{0,2,1:T(8,128)(2,1)S(1)} %bitcast.81, bf16[1024,8,128]{2,0,1:T(8,128)(2,1)} %get-tuple-element.348), kind=kOutput, calls=%fused_computation.2.clone.1 | convolution fusion | flops 1086316544 | bytes 19956224 | tf_op jit(solution)/shard_map/cond/branch_1_fun/while/body/eval_jaxpr/qhd,khd->hqk/dot_general | solution.py:75
  235.3 1.5 constant_dynamic-slice_fusion.9
  236.8 12.0 %bitcast_add_fusion.2 = f32[1024,8,128]{0,2,1:T(8,128)} fusion(f32[1024,8,128]{0,2,1:T(8,128)} %get-tuple-element.333, bf16[512,8,128]{0,2,1:T(8,128)(2,1)S(1)} %bitcast.82, f32[8,512,1024]{2,1,0:T(8,128)} %get-tuple-element.316, f32[8,1024]{1,0:T(8,128)S(1)} %get-tuple-element.343, pred[512]{0:T(512)(128)(4,1)S(1)} %add_compare_fusion.2, ...), kind=kOutput, calls=%fused_computation.11.clone.1 | convolution fusion | flops 1097859072 | bytes 26280448 | tf_op jit(solution)/shard_map/cond/branch_1_fun/while/body/eval_jaxpr/hqk,khd->qhd/dot_general | solution.py:84
  248.8 4.6 fusion.38
  253.5 1.4 fusion.39
  256.7 9.4 %bitcast_reduce_fusion.2 = (f32[8,1024]{1,0:T(8,128)S(1)}, f32[8,512,1024]{2,1,0:T(8,128)}) fusion(pred[512]{0:T(512)(128)(4,1)S(1)} %add_compare_fusion.2, bf16[512,8,128]{0,2,1:T(8,128)(2,1)S(1)} %bitcast.81, bf16[1024,8,128]{2,0,1:T(8,128)(2,1)} %get-tuple-element.348), kind=kOutput, calls=%fused_computation.2.clone.1 | convolution fusion | flops 1086316544 | bytes 19956224 | tf_op jit(solution)/shard_map/cond/branch_1_fun/while/body/eval_jaxpr/qhd,khd->hqk/dot_general | solution.py:75
  266.2 1.5 constant_dynamic-slice_fusion.9
  267.7 12.0 %bitcast_add_fusion.2 = f32[1024,8,128]{0,2,1:T(8,128)} fusion(f32[1024,8,128]{0,2,1:T(8,128)} %get-tuple-element.333, bf16[512,8,128]{0,2,1:T(8,128)(2,1)S(1)} %bitcast.82, f32[8,512,1024]{2,1,0:T(8,128)} %get-tuple-element.316, f32[8,1024]{1,0:T(8,128)S(1)} %get-tuple-element.343, pred[512]{0:T(512)(128)(4,1)S(1)} %add_compare_fusion.2, ...), kind=kOutput, calls=%fused_computation.11.clone.1 | convolution fusion | flops 1097859072 | bytes 26280448 | tf_op jit(solution)/shard_map/cond/branch_1_fun/while/body/eval_jaxpr/hqk,khd->qhd/dot_general | solution.py:84
  279.8 4.6 fusion.38
  284.4 1.4 fusion.39
  287.7 9.4 %bitcast_reduce_fusion.2 = (f32[8,1024]{1,0:T(8,128)S(1)}, f32[8,512,1024]{2,1,0:T(8,128)}) fusion(pred[512]{0:T(512)(128)(4,1)S(1)} %add_compare_fusion.2, bf16[512,8,128]{0,2,1:T(8,128)(2,1)S(1)} %bitcast.81, bf16[1024,8,128]{2,0,1:T(8,128)(2,1)} %get-tuple-element.348), kind=kOutput, calls=%fused_computation.2.clone.1 | convolution fusion | flops 1086316544 | bytes 19956224 | tf_op jit(solution)/shard_map/cond/branch_1_fun/while/body/eval_jaxpr/qhd,khd->hqk/dot_general | solution.py:75
  297.1 1.5 constant_dynamic-slice_fusion.9
  298.6 12.0 %bitcast_add_fusion.2 = f32[1024,8,128]{0,2,1:T(8,128)} fusion(f32[1024,8,128]{0,2,1:T(8,128)} %get-tuple-element.333, bf16[512,8,128]{0,2,1:T(8,128)(2,1)S(1)} %bitcast.82, f32[8,512,1024]{2,1,0:T(8,128)} %get-tuple-element.316, f32[8,1024]{1,0:T(8,128)S(1)} %get-tuple-element.343, pred[512]{0:T(512)(128)(4,1)S(1)} %add_compare_fusion.2, ...), kind=kOutput, calls=%fused_computation.11.clone.1 | convolution fusion | flops 1097859072 | bytes 26280448 | tf_op jit(solution)/shard_map/cond/branch_1_fun/while/body/eval_jaxpr/hqk,khd->qhd/dot_general | solution.py:84
  310.7 4.6 fusion.38
  315.3 1.4 fusion.39
  318.6 9.4 %bitcast_reduce_fusion.2 = (f32[8,1024]{1,0:T(8,128)S(1)}, f32[8,512,1024]{2,1,0:T(8,128)}) fusion(pred[512]{0:T(512)(128)(4,1)S(1)} %add_compare_fusion.2, bf16[512,8,128]{0,2,1:T(8,128)(2,1)S(1)} %bitcast.81, bf16[1024,8,128]{2,0,1:T(8,128)(2,1)} %get-tuple-element.348), kind=kOutput, calls=%fused_computation.2.clone.1 | convolution fusion | flops 1086316544 | bytes 19956224 | tf_op jit(solution)/shard_map/cond/branch_1_fun/while/body/eval_jaxpr/qhd,khd->hqk/dot_general | solution.py:75
  328.0 1.5 constant_dynamic-slice_fusion.9
  329.5 12.0 %bitcast_add_fusion.2 = f32[1024,8,128]{0,2,1:T(8,128)} fusion(f32[1024,8,128]{0,2,1:T(8,128)} %get-tuple-element.333, bf16[512,8,128]{0,2,1:T(8,128)(2,1)S(1)} %bitcast.82, f32[8,512,1024]{2,1,0:T(8,128)} %get-tuple-element.316, f32[8,1024]{1,0:T(8,128)S(1)} %get-tuple-element.343, pred[512]{0:T(512)(128)(4,1)S(1)} %add_compare_fusion.2, ...), kind=kOutput, calls=%fused_computation.11.clone.1 | convolution fusion | flops 1097859072 | bytes 26280448 | tf_op jit(solution)/shard_map/cond/branch_1_fun/while/body/eval_jaxpr/hqk,khd->qhd/dot_general | solution.py:84
  341.6 4.6 fusion.38
  346.3 1.4 fusion.39
  349.5 9.4 %bitcast_reduce_fusion.2 = (f32[8,1024]{1,0:T(8,128)S(1)}, f32[8,512,1024]{2,1,0:T(8,128)}) fusion(pred[512]{0:T(512)(128)(4,1)S(1)} %add_compare_fusion.2, bf16[512,8,128]{0,2,1:T(8,128)(2,1)S(1)} %bitcast.81, bf16[1024,8,128]{2,0,1:T(8,128)(2,1)} %get-tuple-element.348), kind=kOutput, calls=%fused_computation.2.clone.1 | convolution fusion | flops 1086316544 | bytes 19956224 | tf_op jit(solution)/shard_map/cond/branch_1_fun/while/body/eval_jaxpr/qhd,khd->hqk/dot_general | solution.py:75
  359.0 1.5 constant_dynamic-slice_fusion.9
  360.4 12.0 %bitcast_add_fusion.2 = f32[1024,8,128]{0,2,1:T(8,128)} fusion(f32[1024,8,128]{0,2,1:T(8,128)} %get-tuple-element.333, bf16[512,8,128]{0,2,1:T(8,128)(2,1)S(1)} %bitcast.82, f32[8,512,1024]{2,1,0:T(8,128)} %get-tuple-element.316, f32[8,1024]{1,0:T(8,128)S(1)} %get-tuple-element.343, pred[512]{0:T(512)(128)(4,1)S(1)} %add_compare_fusion.2, ...), kind=kOutput, calls=%fused_computation.11.clone.1 | convolution fusion | flops 1097859072 | bytes 26280448 | tf_op jit(solution)/shard_map/cond/branch_1_fun/while/body/eval_jaxpr/hqk,khd->qhd/dot_general | solution.py:84
  372.5 4.6 fusion.38
  377.2 1.4 fusion.39
  380.4 9.4 %bitcast_reduce_fusion.2 = (f32[8,1024]{1,0:T(8,128)S(1)}, f32[8,512,1024]{2,1,0:T(8,128)}) fusion(pred[512]{0:T(512)(128)(4,1)S(1)} %add_compare_fusion.2, bf16[512,8,128]{0,2,1:T(8,128)(2,1)S(1)} %bitcast.81, bf16[1024,8,128]{2,0,1:T(8,128)(2,1)} %get-tuple-element.348), kind=kOutput, calls=%fused_computation.2.clone.1 | convolution fusion | flops 1086316544 | bytes 19956224 | tf_op jit(solution)/shard_map/cond/branch_1_fun/while/body/eval_jaxpr/qhd,khd->hqk/dot_general | solution.py:75
  389.9 1.5 constant_dynamic-slice_fusion.9
  391.4 12.0 %bitcast_add_fusion.2 = f32[1024,8,128]{0,2,1:T(8,128)} fusion(f32[1024,8,128]{0,2,1:T(8,128)} %get-tuple-element.333, bf16[512,8,128]{0,2,1:T(8,128)(2,1)S(1)} %bitcast.82, f32[8,512,1024]{2,1,0:T(8,128)} %get-tuple-element.316, f32[8,1024]{1,0:T(8,128)S(1)} %get-tuple-element.343, pred[512]{0:T(512)(128)(4,1)S(1)} %add_compare_fusion.2, ...), kind=kOutput, calls=%fused_computation.11.clone.1 | convolution fusion | flops 1097859072 | bytes 26280448 | tf_op jit(solution)/shard_map/cond/branch_1_fun/while/body/eval_jaxpr/hqk,khd->qhd/dot_general | solution.py:84
  403.4 4.6 fusion.38
  411.3 9.4 %bitcast_reduce_fusion.2 = (f32[8,1024]{1,0:T(8,128)S(1)}, f32[8,512,1024]{2,1,0:T(8,128)}) fusion(pred[512]{0:T(512)(128)(4,1)S(1)} %add_compare_fusion.2, bf16[512,8,128]{0,2,1:T(8,128)(2,1)S(1)} %bitcast.81, bf16[1024,8,128]{2,0,1:T(8,128)(2,1)} %get-tuple-element.348), kind=kOutput, calls=%fused_computation.2.clone.1 | convolution fusion | flops 1086316544 | bytes 19956224 | tf_op jit(solution)/shard_map/cond/branch_1_fun/while/body/eval_jaxpr/qhd,khd->hqk/dot_general | solution.py:75
  420.8 1.5 constant_dynamic-slice_fusion.9
  422.3 12.0 %bitcast_add_fusion.2 = f32[1024,8,128]{0,2,1:T(8,128)} fusion(f32[1024,8,128]{0,2,1:T(8,128)} %get-tuple-element.333, bf16[512,8,128]{0,2,1:T(8,128)(2,1)S(1)} %bitcast.82, f32[8,512,1024]{2,1,0:T(8,128)} %get-tuple-element.316, f32[8,1024]{1,0:T(8,128)S(1)} %get-tuple-element.343, pred[512]{0:T(512)(128)(4,1)S(1)} %add_compare_fusion.2, ...), kind=kOutput, calls=%fused_computation.11.clone.1 | convolution fusion | flops 1097859072 | bytes 26280448 | tf_op jit(solution)/shard_map/cond/branch_1_fun/while/body/eval_jaxpr/hqk,khd->qhd/dot_general | solution.py:84
  434.4 4.6 fusion.38
  440.4 2.8 divide_convert_fusion
  443.2 2.8 reshape.121
  446.0 4.3 copy.62
  450.3 4.6 all-to-all-start.2
  456.4 47.3 %all-to-all-done.2 = bf16[4,256,1024]{2,1,0:T(8,128)(2,1)} async-done(((bf16[4,256,1024]{2,1,0:T(8,128)(2,1)}), bf16[4,256,1024]{2,1,0:T(8,128)(2,1)}, u32[]{:S(2)}, u32[]{:S(2)}) %all-to-all-start.2) | async-done | bytes 2097184 | tf_op jit(solution)/shard_map/all_to_all | solution.py:101
  503.7 2.8 copy.58
  507.6 2.9 copy.59
  (144 shorter events, 27.4 us)
Async XLA Ops:
  6.5 448.9 %copy-start = (f32[32,4096]{1,0:T(8,128)S(1)}, f32[32,4096]{1,0:T(8,128)}, u32[]{:S(2)}) copy-start(f32[32,4096]{1,0:T(8,128)} %param.13) | copy-start | bytes 1572868
  6.5 176.2 %all-gather.5.cloned.1.call-start = ((), (), s32[]{:S(2)}) async-start(), calls=%async_computation.4 | async-start | bytes 10485760 | tf_op jit(solution)/shard_map/all_gather | solution.py:63
  12.3 39.4 %collective-permute-start.1 = (bf16[256,1024]{1,0:T(8,128)(2,1)S(1)}, bf16[256,1024]{1,0:T(8,128)(2,1)S(1)}, u32[]{:S(2)}, u32[]{:S(2)}) collective-permute-start(bf16[256,1024]{1,0:T(8,128)(2,1)S(1)} %bitcast.93), channel_id=1, source_target_pairs={{0,2},{1,3},{2,0},{3,1},{4,6},{5,7},{6,4},{7,5},{8,10},{9,11},{10,... | collective-permute-start | bytes 1572872 | tf_op jit(solution)/shard_map/ppermute | solution.py:35
  17.7 34.0 %collective-permute-start.2 = (bf16[256,1024]{1,0:T(8,128)(2,1)S(1)}, bf16[256,1024]{1,0:T(8,128)(2,1)}, u32[]{:S(2)}, u32[]{:S(2)}) collective-permute-start(bf16[256,1024]{1,0:T(8,128)(2,1)S(1)} %bitcast.94), channel_id=1, source_target_pairs={{0,3},{1,2},{2,1},{3,0},{4,7},{5,6},{6,5},{7,4},{8,11},{9,10},{10,... | collective-permute-start | bytes 1572872 | tf_op jit(solution)/shard_map/ppermute | solution.py:35
  20.3 34.6 %collective-permute-start = (bf16[256,1024]{1,0:T(8,128)(2,1)S(1)}, bf16[256,1024]{1,0:T(8,128)(2,1)}, u32[]{:S(2)}, u32[]{:S(2)}) collective-permute-start(bf16[256,1024]{1,0:T(8,128)(2,1)S(1)} %bitcast.95), channel_id=1, source_target_pairs={{0,1},{1,0},{2,3},{3,2},{4,5},{5,4},{6,7},{7,6},{8,9},{9,8},{10,11... | collective-permute-start | bytes 1572872 | tf_op jit(solution)/shard_map/ppermute | solution.py:35
  51.7 3.2 copy-start.2
  58.7 4.2 copy-start.1
  62.8 125.9 %all-gather.3.cloned.1.call-start = ((), (), s32[]{:S(2)}) async-start(), calls=%async_computation.3 | async-start | bytes 10485760 | tf_op jit(solution)/shard_map/all_gather | solution.py:62
  131.5 51.3 %all-to-all-start = ((bf16[256,4,1024]{0,2,1:T(8,128)(2,1)}), bf16[256,4,1024]{0,2,1:T(8,128)(2,1)S(1)}, u32[]{:S(2)}, u32[]{:S(2)}) async-start(bf16[256,4,1024]{0,2,1:T(8,128)(2,1)} %bitcast.86), calls=%async_computation | async-start | bytes 4194304 | tf_op jit(solution)/shard_map/all_to_all | solution.py:46
  206.3 12.4 %slice-start = ((s8[16777216]{0:T(1024)(128)(4,1)}), s8[4194304]{0:T(1024)(128)(4,1)S(1)}, s32[]{:S(2)}) async-start(s8[16777216]{0:T(1024)(128)(4,1)} %bitcast.79), calls=%async_computation.5 | async-start | bytes 8388608 | tf_op jit(solution)/shard_map/cond/branch_1_fun/while
  207.7 10.9 %slice-start.1 = ((s8[16777216]{0:T(1024)(128)(4,1)}), s8[4194304]{0:T(1024)(128)(4,1)S(1)}, s32[]{:S(2)}) async-start(s8[16777216]{0:T(1024)(128)(4,1)} %bitcast.79), calls=%async_computation.6 | async-start | bytes 8388608 | tf_op jit(solution)/shard_map/cond/branch_1_fun/while
  207.8 10.9 %slice-start.2 = ((s8[16777216]{0:T(1024)(128)(4,1)}), s8[4194304]{0:T(1024)(128)(4,1)S(1)}, s32[]{:S(2)}) async-start(s8[16777216]{0:T(1024)(128)(4,1)} %bitcast.79), calls=%async_computation.7 | async-start | bytes 8388608 | tf_op jit(solution)/shard_map/cond/branch_1_fun/while
  207.8 10.9 %slice-start.3 = ((s8[16777216]{0:T(1024)(128)(4,1)}), s8[4194304]{0:T(1024)(128)(4,1)S(1)}, s32[]{:S(2)}) async-start(s8[16777216]{0:T(1024)(128)(4,1)} %bitcast.79), calls=%async_computation.8 | async-start | bytes 8388608 | tf_op jit(solution)/shard_map/cond/branch_1_fun/while
  235.3 13.5 %slice-start = ((s8[16777216]{0:T(1024)(128)(4,1)}), s8[4194304]{0:T(1024)(128)(4,1)S(1)}, s32[]{:S(2)}) async-start(s8[16777216]{0:T(1024)(128)(4,1)} %bitcast.79), calls=%async_computation.5 | async-start | bytes 8388608 | tf_op jit(solution)/shard_map/cond/branch_1_fun/while
  236.7 12.1 %slice-start.1 = ((s8[16777216]{0:T(1024)(128)(4,1)}), s8[4194304]{0:T(1024)(128)(4,1)S(1)}, s32[]{:S(2)}) async-start(s8[16777216]{0:T(1024)(128)(4,1)} %bitcast.79), calls=%async_computation.6 | async-start | bytes 8388608 | tf_op jit(solution)/shard_map/cond/branch_1_fun/while
  236.7 12.1 %slice-start.2 = ((s8[16777216]{0:T(1024)(128)(4,1)}), s8[4194304]{0:T(1024)(128)(4,1)S(1)}, s32[]{:S(2)}) async-start(s8[16777216]{0:T(1024)(128)(4,1)} %bitcast.79), calls=%async_computation.7 | async-start | bytes 8388608 | tf_op jit(solution)/shard_map/cond/branch_1_fun/while
  236.7 12.1 %slice-start.3 = ((s8[16777216]{0:T(1024)(128)(4,1)}), s8[4194304]{0:T(1024)(128)(4,1)S(1)}, s32[]{:S(2)}) async-start(s8[16777216]{0:T(1024)(128)(4,1)} %bitcast.79), calls=%async_computation.8 | async-start | bytes 8388608 | tf_op jit(solution)/shard_map/cond/branch_1_fun/while
  266.2 13.5 %slice-start = ((s8[16777216]{0:T(1024)(128)(4,1)}), s8[4194304]{0:T(1024)(128)(4,1)S(1)}, s32[]{:S(2)}) async-start(s8[16777216]{0:T(1024)(128)(4,1)} %bitcast.79), calls=%async_computation.5 | async-start | bytes 8388608 | tf_op jit(solution)/shard_map/cond/branch_1_fun/while
  267.6 12.1 %slice-start.1 = ((s8[16777216]{0:T(1024)(128)(4,1)}), s8[4194304]{0:T(1024)(128)(4,1)S(1)}, s32[]{:S(2)}) async-start(s8[16777216]{0:T(1024)(128)(4,1)} %bitcast.79), calls=%async_computation.6 | async-start | bytes 8388608 | tf_op jit(solution)/shard_map/cond/branch_1_fun/while
  267.7 12.1 %slice-start.2 = ((s8[16777216]{0:T(1024)(128)(4,1)}), s8[4194304]{0:T(1024)(128)(4,1)S(1)}, s32[]{:S(2)}) async-start(s8[16777216]{0:T(1024)(128)(4,1)} %bitcast.79), calls=%async_computation.7 | async-start | bytes 8388608 | tf_op jit(solution)/shard_map/cond/branch_1_fun/while
  267.7 12.1 %slice-start.3 = ((s8[16777216]{0:T(1024)(128)(4,1)}), s8[4194304]{0:T(1024)(128)(4,1)S(1)}, s32[]{:S(2)}) async-start(s8[16777216]{0:T(1024)(128)(4,1)} %bitcast.79), calls=%async_computation.8 | async-start | bytes 8388608 | tf_op jit(solution)/shard_map/cond/branch_1_fun/while
  297.1 13.5 %slice-start = ((s8[16777216]{0:T(1024)(128)(4,1)}), s8[4194304]{0:T(1024)(128)(4,1)S(1)}, s32[]{:S(2)}) async-start(s8[16777216]{0:T(1024)(128)(4,1)} %bitcast.79), calls=%async_computation.5 | async-start | bytes 8388608 | tf_op jit(solution)/shard_map/cond/branch_1_fun/while
  298.6 12.1 %slice-start.1 = ((s8[16777216]{0:T(1024)(128)(4,1)}), s8[4194304]{0:T(1024)(128)(4,1)S(1)}, s32[]{:S(2)}) async-start(s8[16777216]{0:T(1024)(128)(4,1)} %bitcast.79), calls=%async_computation.6 | async-start | bytes 8388608 | tf_op jit(solution)/shard_map/cond/branch_1_fun/while
  298.6 12.1 %slice-start.2 = ((s8[16777216]{0:T(1024)(128)(4,1)}), s8[4194304]{0:T(1024)(128)(4,1)S(1)}, s32[]{:S(2)}) async-start(s8[16777216]{0:T(1024)(128)(4,1)} %bitcast.79), calls=%async_computation.7 | async-start | bytes 8388608 | tf_op jit(solution)/shard_map/cond/branch_1_fun/while
  298.6 12.1 %slice-start.3 = ((s8[16777216]{0:T(1024)(128)(4,1)}), s8[4194304]{0:T(1024)(128)(4,1)S(1)}, s32[]{:S(2)}) async-start(s8[16777216]{0:T(1024)(128)(4,1)} %bitcast.79), calls=%async_computation.8 | async-start | bytes 8388608 | tf_op jit(solution)/shard_map/cond/branch_1_fun/while
  328.0 13.5 %slice-start = ((s8[16777216]{0:T(1024)(128)(4,1)}), s8[4194304]{0:T(1024)(128)(4,1)S(1)}, s32[]{:S(2)}) async-start(s8[16777216]{0:T(1024)(128)(4,1)} %bitcast.79), calls=%async_computation.5 | async-start | bytes 8388608 | tf_op jit(solution)/shard_map/cond/branch_1_fun/while
  329.5 12.1 %slice-start.1 = ((s8[16777216]{0:T(1024)(128)(4,1)}), s8[4194304]{0:T(1024)(128)(4,1)S(1)}, s32[]{:S(2)}) async-start(s8[16777216]{0:T(1024)(128)(4,1)} %bitcast.79), calls=%async_computation.6 | async-start | bytes 8388608 | tf_op jit(solution)/shard_map/cond/branch_1_fun/while
  329.5 12.1 %slice-start.2 = ((s8[16777216]{0:T(1024)(128)(4,1)}), s8[4194304]{0:T(1024)(128)(4,1)S(1)}, s32[]{:S(2)}) async-start(s8[16777216]{0:T(1024)(128)(4,1)} %bitcast.79), calls=%async_computation.7 | async-start | bytes 8388608 | tf_op jit(solution)/shard_map/cond/branch_1_fun/while
  329.5 12.1 %slice-start.3 = ((s8[16777216]{0:T(1024)(128)(4,1)}), s8[4194304]{0:T(1024)(128)(4,1)S(1)}, s32[]{:S(2)}) async-start(s8[16777216]{0:T(1024)(128)(4,1)} %bitcast.79), calls=%async_computation.8 | async-start | bytes 8388608 | tf_op jit(solution)/shard_map/cond/branch_1_fun/while
  358.9 13.5 %slice-start = ((s8[16777216]{0:T(1024)(128)(4,1)}), s8[4194304]{0:T(1024)(128)(4,1)S(1)}, s32[]{:S(2)}) async-start(s8[16777216]{0:T(1024)(128)(4,1)} %bitcast.79), calls=%async_computation.5 | async-start | bytes 8388608 | tf_op jit(solution)/shard_map/cond/branch_1_fun/while
  360.4 12.1 %slice-start.1 = ((s8[16777216]{0:T(1024)(128)(4,1)}), s8[4194304]{0:T(1024)(128)(4,1)S(1)}, s32[]{:S(2)}) async-start(s8[16777216]{0:T(1024)(128)(4,1)} %bitcast.79), calls=%async_computation.6 | async-start | bytes 8388608 | tf_op jit(solution)/shard_map/cond/branch_1_fun/while
  360.4 12.1 %slice-start.2 = ((s8[16777216]{0:T(1024)(128)(4,1)}), s8[4194304]{0:T(1024)(128)(4,1)S(1)}, s32[]{:S(2)}) async-start(s8[16777216]{0:T(1024)(128)(4,1)} %bitcast.79), calls=%async_computation.7 | async-start | bytes 8388608 | tf_op jit(solution)/shard_map/cond/branch_1_fun/while
  360.4 12.1 %slice-start.3 = ((s8[16777216]{0:T(1024)(128)(4,1)}), s8[4194304]{0:T(1024)(128)(4,1)S(1)}, s32[]{:S(2)}) async-start(s8[16777216]{0:T(1024)(128)(4,1)} %bitcast.79), calls=%async_computation.8 | async-start | bytes 8388608 | tf_op jit(solution)/shard_map/cond/branch_1_fun/while
  389.9 13.5 %slice-start = ((s8[16777216]{0:T(1024)(128)(4,1)}), s8[4194304]{0:T(1024)(128)(4,1)S(1)}, s32[]{:S(2)}) async-start(s8[16777216]{0:T(1024)(128)(4,1)} %bitcast.79), calls=%async_computation.5 | async-start | bytes 8388608 | tf_op jit(solution)/shard_map/cond/branch_1_fun/while
  391.3 12.1 %slice-start.1 = ((s8[16777216]{0:T(1024)(128)(4,1)}), s8[4194304]{0:T(1024)(128)(4,1)S(1)}, s32[]{:S(2)}) async-start(s8[16777216]{0:T(1024)(128)(4,1)} %bitcast.79), calls=%async_computation.6 | async-start | bytes 8388608 | tf_op jit(solution)/shard_map/cond/branch_1_fun/while
  391.3 12.1 %slice-start.2 = ((s8[16777216]{0:T(1024)(128)(4,1)}), s8[4194304]{0:T(1024)(128)(4,1)S(1)}, s32[]{:S(2)}) async-start(s8[16777216]{0:T(1024)(128)(4,1)} %bitcast.79), calls=%async_computation.7 | async-start | bytes 8388608 | tf_op jit(solution)/shard_map/cond/branch_1_fun/while
  391.4 12.1 %slice-start.3 = ((s8[16777216]{0:T(1024)(128)(4,1)}), s8[4194304]{0:T(1024)(128)(4,1)S(1)}, s32[]{:S(2)}) async-start(s8[16777216]{0:T(1024)(128)(4,1)} %bitcast.79), calls=%async_computation.8 | async-start | bytes 8388608 | tf_op jit(solution)/shard_map/cond/branch_1_fun/while
  420.8 13.5 %slice-start = ((s8[16777216]{0:T(1024)(128)(4,1)}), s8[4194304]{0:T(1024)(128)(4,1)S(1)}, s32[]{:S(2)}) async-start(s8[16777216]{0:T(1024)(128)(4,1)} %bitcast.79), calls=%async_computation.5 | async-start | bytes 8388608 | tf_op jit(solution)/shard_map/cond/branch_1_fun/while
  422.3 12.1 %slice-start.1 = ((s8[16777216]{0:T(1024)(128)(4,1)}), s8[4194304]{0:T(1024)(128)(4,1)S(1)}, s32[]{:S(2)}) async-start(s8[16777216]{0:T(1024)(128)(4,1)} %bitcast.79), calls=%async_computation.6 | async-start | bytes 8388608 | tf_op jit(solution)/shard_map/cond/branch_1_fun/while
  422.3 12.1 %slice-start.2 = ((s8[16777216]{0:T(1024)(128)(4,1)}), s8[4194304]{0:T(1024)(128)(4,1)S(1)}, s32[]{:S(2)}) async-start(s8[16777216]{0:T(1024)(128)(4,1)} %bitcast.79), calls=%async_computation.7 | async-start | bytes 8388608 | tf_op jit(solution)/shard_map/cond/branch_1_fun/while
  422.3 12.1 %slice-start.3 = ((s8[16777216]{0:T(1024)(128)(4,1)}), s8[4194304]{0:T(1024)(128)(4,1)S(1)}, s32[]{:S(2)}) async-start(s8[16777216]{0:T(1024)(128)(4,1)} %bitcast.79), calls=%async_computation.8 | async-start | bytes 8388608 | tf_op jit(solution)/shard_map/cond/branch_1_fun/while
  446.0 8.9 %copy-start.3 = (s32[4]{0:T(128)S(1)}, s32[4]{0:T(128)}, u32[]{:S(2)}) copy-start(s32[4]{0:T(128)} %param.12) | copy-start | bytes 52
  450.3 53.4 %all-to-all-start.2 = ((bf16[4,256,1024]{2,1,0:T(8,128)(2,1)}), bf16[4,256,1024]{2,1,0:T(8,128)(2,1)}, u32[]{:S(2)}, u32[]{:S(2)}) async-start(bf16[4,256,1024]{2,1,0:T(8,128)(2,1)} %copy.62), calls=%async_computation.2 | async-start | bytes 4194304 | tf_op jit(solution)/shard_map/all_to_all | solution.py:101
Sparse Core Ops, SparseCore 0:
  62.9 65.8 all-gather.4
  130.4 58.2 all-gather.2
